TPU v7x, 128 devices: a whole 4x4x4 slice. The times are simulated.
128 devices in a mesh: st: 16 (over x, z_lo, core), hr: 8 (over z_hi, y).
Axes of the slice: x: 4, y: 4, z: 4 (z_hi: 2, z_lo: 2; z = z_hi * 2 + z_lo), core: 2. Of those that a mesh axis runs over, the one named last changes fastest.
Arguments:
- cotangent: bfloat16 [256, 64, 4096], P('hr', None, 'st'), may hold values from -24 to 24
- field: bfloat16 [256, 64, 4096], P('hr', None, 'st'), may hold values from -1.5 to 1.5
- temporal: bfloat16 [256, 256], replicated, may hold values from -0.375 to 0.375
- embed: float32 [16, 4096], P(None, 'st'), may hold values from -5 to 5
Outputs:
- field_grad: bfloat16 [256, 64, 4096], P('hr', None, 'st')
- embed_grad: float32 [16, 4096], P(None, 'st')
All inputs are finite; a program needn't handle non-finite values.
Results may differ from a plain program's by a relative error of at most 0.02.
Values may be sent and summed in bfloat16 or wider, within the bound.
A program may use at most 128 MiB of HBM per device.

v0:
```python
import math

import jax
import jax.numpy as jnp
from jax import lax
from jax.sharding import PartitionSpec as P

HIGHEST = lax.Precision.HIGHEST


def kernel_tile(emb_left, emb_right, amplitude):
    cross_term = lax.dot_general(emb_left, emb_right, (((0,), (0,)), ((), ())), precision=HIGHEST)
    norm_left = jnp.sum(emb_left * emb_left, axis=0)
    norm_right = jnp.sum(emb_right * emb_right, axis=0)
    distance = norm_left[:, None] + norm_right[None, :] - 2.0 * cross_term
    return jnp.exp(distance * (-0.5 / emb_left.shape[0])) * amplitude


def add_columns(far_acc, update, offset):
    length = update.shape[1]
    current = lax.dynamic_slice_in_dim(far_acc, offset, length, 1)
    return lax.dynamic_update_slice_in_dim(far_acc, current + update, offset, 1)


def on_device(cotangent, field, temporal, embed):
    hours_dev, chans, st_rows = cotangent.shape
    emb_width = embed.shape[0]
    total = st_rows * lax.axis_size("st")
    amplitude = 1.0 / math.sqrt(total)
    hour_offset = lax.axis_index("hr") * hours_dev
    kt_cols = lax.dynamic_slice_in_dim(temporal, hour_offset, hours_dev, 1)
    cot_piece = lax.all_gather(cotangent, "hr", axis=0, tiled=True)
    length = cot_piece.shape[0]
    cot_flat = cot_piece.reshape(length, chans * st_rows)
    mixed_cot = lax.dot_general(
        kt_cols, cot_flat, (((0,), (0,)), ((), ())), preferred_element_type=jnp.float32
    )
    mixed_cot = mixed_cot.astype(jnp.bfloat16).reshape(hours_dev * chans, st_rows)
    field_flat = field.reshape(hours_dev * chans, st_rows)
    own_init = jnp.zeros((emb_width, st_rows), jnp.float32)
    far_init = jnp.zeros((emb_width, total), jnp.float32)
    cot_piece = lax.all_gather(mixed_cot, "st", axis=1, tiled=True)
    emb_piece = lax.all_gather(embed.astype(jnp.bfloat16), "st", axis=1, tiled=True).astype(
        jnp.float32
    )
    ker_tile = kernel_tile(embed, emb_piece, amplitude)
    grad_acc = lax.dot_general(
        cot_piece,
        ker_tile.astype(jnp.bfloat16),
        (((1,), (1,)), ((), ())),
        preferred_element_type=jnp.float32,
    )
    own_acc = own_init
    far_acc = far_init
    field_piece = lax.all_gather(field_flat, "st", axis=1, tiled=True)
    emb_piece = lax.all_gather(embed.astype(jnp.bfloat16), "st", axis=1, tiled=True).astype(
        jnp.float32
    )
    ker_tile = kernel_tile(emb_piece, embed, amplitude)
    gram = lax.dot_general(
        field_piece, mixed_cot, (((0,), (0,)), ((), ())), preferred_element_type=jnp.float32
    )
    weight = gram * ker_tile
    far_part = lax.dot_general(embed, weight, (((1,), (1,)), ((), ())), precision=HIGHEST)
    far_part = far_part - emb_piece * jnp.sum(weight, axis=1)[None, :]
    far_acc = add_columns(far_acc, far_part, jnp.int32(0))
    own_part = jnp.dot(emb_piece, weight, precision=HIGHEST)
    own_acc = own_acc + own_part - embed * jnp.sum(weight, axis=0)[None, :]
    own_acc, far_acc = (own_acc, far_acc)
    far_acc = add_columns(far_acc, own_acc, lax.axis_index("st") * st_rows)
    far_acc = far_acc * (1.0 / emb_width)
    shares = lax.psum_scatter(
        far_acc.astype(jnp.bfloat16), "st", scatter_dimension=1, tiled=True
    ).astype(jnp.float32)
    embed_grad = lax.psum(shares, "hr")
    field_grad = grad_acc.astype(jnp.bfloat16).reshape(hours_dev, chans, st_rows)
    return (field_grad, embed_grad)


def solution(mesh):
    return jax.shard_map(
        on_device,
        mesh=mesh,
        in_specs=(P("hr", None, "st"), P("hr", None, "st"), P(), P(None, "st")),
        out_specs=(P("hr", None, "st"), P(None, "st")),
        check_vma=False,
    )
```

profile of v0, /device:TPU:0, one launch (start us, length us, event | category | flops | bytes accessed | tf_op | source)
XLA Modules:
  0.0 416.5 jit_solution(12895805128267997930)
XLA Ops:
  7.2 0.0 copy-start
  7.2 0.0 all-gather.4.cloned.1.call-start
  7.2 0.7 all-gather.4.cloned.1.call-update
  7.9 0.0 all-gather.8.cloned.1.call-start
  8.0 0.7 all-gather.8.cloned.1.call-update
  8.7 0.0 reduce-scatter.2.cloned.1.call-start
  8.7 0.8 multiply_reduce_fusion
  9.5 20.6 %all_gather.15 = bf16[16,4096]{1,0:T(8,128)(2,1)S(1)} all-gather(bf16[16,256]{1,0:T(8,128)(2,1)S(1)} %get-tuple-element.5), channel_id=1, replica_groups=mesh['st'=16,'hr'=8] {'st'}, dimensions={1}, use_global_device_ids=true | all-gather | bytes 139264 | tf_op jit(solution)/shard_map/all_gather | solution.py:43
  30.1 0.1 fusion.14
  30.1 5.4 %fusion.3 = f32[4096,256]{0,1:T(8,128)} fusion(bf16[16,4096]{1,0:T(8,128)(2,1)S(1)} %all_gather.15, f32[16,256]{1,0:T(8,128)} %param.7, f32[256]{0:T(256)S(1)} %get-tuple-element.4, f32[4096]{0:T(1024)S(1)} %fusion.14), kind=kOutput, calls=%fused_computation.5 | convolution fusion | flops 206569472 | bytes 4359168 | tf_op jit(solution)/shard_map/dot_general | solution.py:12
  35.5 86.3 %all-gather.4.cloned.1.call-done = bf16[256,64,256]{2,1,0:T(8,128)(2,1)} async-done(((bf16[32,64,256]{2,1,0:T(8,128)(2,1)}), bf16[256,64,256]{2,1,0:T(8,128)(2,1)}) %all-gather.4.cloned.1.call-update) | async-done | bytes 8388624 | tf_op jit(solution)/shard_map/all_gather | solution.py:32
  121.8 15.2 %copy.9 = bf16[32,8,64,256]{3,1,2,0:T(8,128)(2,1)} copy(bf16[32,8,64,256]{3,2,1,0:T(8,128)(2,1)} %bitcast.34) | data formatting | bytes 16777216
  137.1 0.0 copy-done
  137.1 5.2 %convolution_convert_fusion = bf16[32,16384]{1,0:T(8,128)(2,1)S(1)} fusion(bf16[256,16384]{1,0:T(8,128)(2,1)} %bitcast.33, bf16[256,256]{1,0:T(8,128)(2,1)S(1)} %copy-done, s32[]{:T(128)S(6)} %select_n.7), kind=kOutput, calls=%fused_computation | convolution fusion | flops 268959744 | bytes 9502724 | tf_op jit(solution)/shard_map/dot_general | solution.py:35
  142.3 0.5 reshape.23
  142.8 0.0 copy-start.1
  142.8 0.0 copy-start.2
  142.8 77.5 %all-gather.8.cloned.1.call-done = bf16[2048,4096]{1,0:T(8,128)(2,1)} async-done(((bf16[2048,256]{1,0:T(8,128)(2,1)}), bf16[2048,4096]{1,0:T(8,128)(2,1)}) %all-gather.8.cloned.1.call-update) | async-done | bytes 16777232 | tf_op jit(solution)/shard_map/all_gather | solution.py:55
  220.3 11.6 %fusion.17 = (f32[256]{0:T(256)S(1)}, f32[4096]{0:T(1024)S(1)}, f32[4096,256]{0,1:T(8,128)S(1)}) fusion(f32[4096,256]{0,1:T(8,128)} %fusion.3, bf16[2048,256]{1,0:T(8,128)(2,1)S(1)} %reshape.23, bf16[2048,4096]{1,0:T(8,128)(2,1)} %all-gather.8.cloned.1.call-done), kind=kOutput, calls=%fused_computation.28 | convolution fusion | flops 4298108928 | bytes 26231808 | tf_op jit(solution)/shard_map/dot_general | solution.py:60
  231.9 0.0 copy-done.1
  231.9 0.0 copy-done.2
  231.9 2.3 fusion.10
  234.2 2.0 fusion.13
  236.2 0.7 multiply_convert_fusion
  236.9 0.0 reduce-scatter.2.cloned.1.call-update
  236.9 0.0 all-gather.6.cloned.1.call-start
  236.9 0.5 all-gather.6.cloned.1.call-update
  237.5 4.1 fusion.9
  241.6 56.1 %reduce-scatter.2.cloned.1.call-done = bf16[16,256]{1,0:T(8,128)(2,1)} async-done(((bf16[16,4096]{1,0:T(8,128)(2,1)}), bf16[16,256]{1,0:T(8,128)(2,1)}) %reduce-scatter.2.cloned.1.call-update) | async-done | bytes 8208 | tf_op jit(solution)/shard_map/reduce_scatter | solution.py:72
  297.7 42.8 %psum.7 = f32[16,256]{1,0:T(8,128)} all-reduce(bf16[16,256]{1,0:T(8,128)(2,1)} %reduce-scatter.2.cloned.1.call-done), channel_id=1, replica_groups=mesh['st'=16,'hr'=8] {'hr'}, use_global_device_ids=true, to_apply=%region_5.0 | all-reduce | flops 4096 | bytes 24576 | tf_op jit(solution)/shard_map/psum | solution.py:75
  340.5 57.4 %all-gather.6.cloned.1.call-done = bf16[2048,4096]{1,0:T(8,128)(2,1)} async-done(((bf16[2048,256]{1,0:T(8,128)(2,1)}), bf16[2048,4096]{1,0:T(8,128)(2,1)}) %all-gather.6.cloned.1.call-update) | async-done | bytes 16777232 | tf_op jit(solution)/shard_map/all_gather | solution.py:42
  397.9 12.1 %convolution_convert_fusion.1 = bf16[2048,256]{1,0:T(8,128)(2,1)} fusion(bf16[2048,4096]{1,0:T(8,128)(2,1)} %all-gather.6.cloned.1.call-done, bf16[256,4096]{1,0:T(8,128)(2,1)} %fusion.9), kind=kOutput, calls=%fused_computation.16 | convolution fusion | flops 4295491584 | bytes 19922944 | tf_op jit(solution)/shard_map/dot_general | solution.py:47
Async XLA Ops:
  7.2 129.9 %copy-start = (bf16[256,256]{1,0:T(8,128)(2,1)S(1)}, bf16[256,256]{1,0:T(8,128)(2,1)}, u32[]{:S(2)}) copy-start(bf16[256,256]{1,0:T(8,128)(2,1)} %param.6) | copy-start | bytes 393220
  7.2 114.7 %all-gather.4.cloned.1.call-start = ((), (), s32[]{:S(2)}) async-start(), calls=%async_computation.1 | async-start | bytes 9437184 | tf_op jit(solution)/shard_map/all_gather | solution.py:32
  7.9 212.4 %all-gather.8.cloned.1.call-start = ((), (), s32[]{:S(2)}) async-start(), calls=%async_computation.3 | async-start | bytes 17825792 | tf_op jit(solution)/shard_map/all_gather | solution.py:55
  8.7 289.0 %reduce-scatter.2.cloned.1.call-start = ((), (), s32[]{:S(2)}) async-start(), calls=%async_computation.4 | async-start | bytes 139264 | tf_op jit(solution)/shard_map/reduce_scatter | solution.py:72
  142.8 89.1 %copy-start.1 = (bf16[2048,256]{1,0:T(8,128)(2,1)}, bf16[2048,256]{1,0:T(8,128)(2,1)S(1)}, u32[]{:S(2)}) copy-start(bf16[2048,256]{1,0:T(8,128)(2,1)S(1)} %reshape.23) | copy-start | bytes 3145732
  142.8 89.1 %copy-start.2 = (f32[16,256]{1,0:T(8,128)S(1)}, f32[16,256]{1,0:T(8,128)}, u32[]{:S(2)}) copy-start(f32[16,256]{1,0:T(8,128)} %param.7) | copy-start | bytes 49156
  236.9 161.0 %all-gather.6.cloned.1.call-start = ((), (), s32[]{:S(2)}) async-start(), calls=%async_computation.2 | async-start | bytes 17825792 | tf_op jit(solution)/shard_map/all_gather | solution.py:42
Sparse Core Ops, SparseCore 0:
  10.3 111.4 all-gather.3
  123.5 96.7 all-gather.7
  237.0 60.6 reduce-scatter.1
  299.8 98.0 all-gather.5
where the time goes:
time: 418 us; the launch traced here: 417 us
  waiting for transfers between devices  279 us (67%)
  blocking collectives  63.4 us (15%)
  matrix products  42.6 us (10%)
  local copies, waits for them, and re-layouts  15.8 us (4%)
  between operations  13.8 us (3%)
    all_gather x1, waiting for transfers between devices, on_device(): cot_piece = lax.all_gather(cotangent, 'hr', axis=0, tiled=True)  86.3 us
    all_gather x1, waiting for transfers between devices, on_device(): field_piece = lax.all_gather(field_flat, 'st', axis=1, tiled=True)  77.5 us
    all_gather x1, waiting for transfers between devices, on_device(): cot_piece = lax.all_gather(mixed_cot, 'st', axis=1, tiled=True)  57.4 us
    reduce_scatter x1, waiting for transfers between devices, on_device(): lax.psum_scatter(far_acc.astype(jnp.bfloat16), 'st', scatter_dimension=1,...  56.1 us
    psum x1, blocking collectives, on_device(): embed_grad = lax.psum(shares, 'hr')  42.8 us
    all_gather x1, blocking collectives, on_device(): lax.all_gather(embed.astype(jnp.bfloat16), 'st', axis=1, tiled=True)  20.6 us
    unnamed x7, local copies, waits for them, and re-layouts  15.2 us
    dot_general x1, matrix products, on_device(): lax.dot_general(cot_piece, ker_tile.astype(jnp.bfloat16), (((1,), (1,)),...  12.1 us
  transfers between devices with their start and end apart: 4, of which 4 were waited for; matrix products, arithmetic and copies ran while one was open for 8% of the time, Pallas kernels for 0%

commit v1 on v0

v1 whole, which is shorter than its diff:
```python
import math

import jax
import jax.numpy as jnp
from jax import lax
from jax.experimental import pallas as pl
from jax.experimental.pallas import tpu as pltpu
from jax.sharding import PartitionSpec as P

F32 = jnp.float32
BF16 = jnp.bfloat16
MESH = pl.DeviceIdType.MESH
LOG2E = 1.0 / math.log(2.0)


def contract(a, b, dim_a, dim_b):
    return lax.dot_general(a, b, (((dim_a,), (dim_b,)), ((), ())), preferred_element_type=F32)


def split3(v):
    high = v.astype(BF16)
    rest = v - high.astype(F32)
    mid = rest.astype(BF16)
    low = (rest - mid.astype(F32)).astype(BF16)
    return high, mid, low


def one_hot_matrix(keep):
    row = lax.broadcasted_iota(jnp.int32, (256, 256), 0)
    col = lax.broadcasted_iota(jnp.int32, (256, 256), 1)
    return jnp.where(keep(row, col), 1.0, 0.0).astype(BF16)


def swap_rows():
    return one_hot_matrix(lambda r, c: ((r >> 4) == (c & 15)) & ((r & 15) == (c >> 4)))


def identity():
    return one_hot_matrix(lambda r, c: r == c)


def swap_leading(src, dst, perm):
    n_a, n_b, width = src.shape
    for b in range(0, n_b, 16):
        for a in range(0, n_a, 16):
            tile = src[a : a + 16, b : b + 16, :].reshape(256, width)
            moved = contract(perm, tile, 1, 0).astype(BF16)
            dst[b : b + 16, a : a + 16, :] = moved.reshape(16, 16, width)


def norm_rows(sq, left, amp_log2):
    parts = [p.astype(F32) for p in split3(sq * (-LOG2E / 32.0) + amp_log2)]
    row = lax.broadcasted_iota(jnp.int32, (16, sq.shape[1]), 0)
    own = 0 if left else 3
    ones = 3 - own
    out = jnp.where((row >= ones) & (row < ones + 3), 1.0, 0.0)
    for q in range(3):
        out = jnp.where(row == own + q, parts[q], out)
    return out.astype(BF16)


def features(e, left, amp_log2):
    sq = jnp.sum(e * e, axis=0, keepdims=True)
    zero = jnp.zeros(e.shape, BF16)
    if left:
        h, m, l = split3(e * (LOG2E / 16.0))
        rows = [h, h, h, norm_rows(sq, True, amp_log2), m, m, l, zero]
    else:
        h, m, l = split3(e)
        rows = [h, m, l, norm_rows(sq, False, 0.0), h, m, h, zero]
    return jnp.concatenate([r.astype(F32) for r in rows], axis=0).astype(BF16)


def kernel(
    cot, field, temporal, embed, grad, egrad,
    raw, fraw, sent, fsent, crecv, pair, tile, left, feat_l, feat_r,
    eall, tmix, osend, orecv, esend, erecv,
    in_sem, send_sem, recv_sem,
):
    st = lax.axis_index("st")
    hr = lax.axis_index("hr")
    core = lax.rem(st, 2)
    col = st // 2
    me = hr * 8 + col
    x, z, y = st // 4, (hr // 4) * 2 + lax.rem(col, 2), lax.rem(hr, 4)
    partner = (st + 1 - 2 * core, hr)

    def peer(k):
        px = lax.rem(x + lax.rem(k, 4), 4)
        py = lax.rem(y + lax.rem(k // 4, 4), 4)
        pz = lax.rem(z + k // 16, 4)
        return px * 2 + lax.rem(pz, 2), (pz // 2) * 4 + py

    def load(i, src, dst):
        return pltpu.make_async_copy(src, dst, in_sem.at[i])

    load(0, cot, raw).start()
    load(1, field, fraw).start()

    barrier = pltpu.get_barrier_semaphore()

    @pl.loop(1, 64)
    def _(k):
        c, h = peer(k)
        pl.semaphore_signal(barrier, inc=1, device_id=(c * 2 + core, h), device_id_type=MESH)

    @pl.loop(0, 8)
    def _(c):
        pl.semaphore_signal(barrier, inc=1, device_id=(c * 2 + 1 - core, hr), device_id_type=MESH)

    perm = swap_rows()
    load(0, cot, raw).wait()
    swap_leading(raw, sent, perm)
    pl.semaphore_wait(barrier, 71)

    def push(i, src, dst, device):
        pltpu.make_async_remote_copy(
            src_ref=src, dst_ref=dst, send_sem=send_sem.at[i], recv_sem=recv_sem.at[i],
            device_id=device, device_id_type=MESH,
        ).start()

    def keep(i, src, dst):
        pltpu.make_async_copy(src, dst, recv_sem.at[i]).start()

    def settle(sem, ref):
        pltpu.make_async_copy(ref, ref, sem).wait()

    @pl.loop(1, 8)
    def _(k):
        c = lax.rem(col + k, 8)
        push(0, embed, eall.at[0, col], (c * 2 + core, hr))

    @pl.loop(0, 8)
    def _(k):
        c = lax.rem(col + k, 8)
        push(0, embed, eall.at[1, col], (c * 2 + 1 - core, hr))

    keep(0, embed, eall.at[0, col])

    @pl.loop(1, 64)
    def _(k):
        c, h = peer(k)
        push(1, sent.at[h * 8 + c], crecv.at[col, hr], (c * 2 + core, h))

    keep(1, sent.at[me], crecv.at[col, hr])

    load(1, field, fraw).wait()
    swap_leading(fraw, fsent, perm)
    hours = pl.ds(pl.multiple_of(256 + hr * 32, 32), 32)

    @pl.loop(1, 64)
    def _(k):
        c, h = peer(k)
        push(2, fsent.at[h * 8 + c], pair.at[0, col, hours, :], (c * 2 + core, h))

    keep(2, fsent.at[me], pair.at[0, col, hours, :])

    eye = identity()
    tmix[...] = contract(eye, temporal[...], 1, 1).astype(BF16)
    amp_log2 = -0.5 * math.log2(4096.0)
    settle(recv_sem.at[0], eall)

    @pl.loop(0, 8)
    def _(a):
        e = eall[0, a]
        feat_l[a] = contract(eye, features(e, True, amp_log2), 1, 1).astype(BF16)
        feat_r[0, a] = features(e, False, 0.0)
        feat_r[1, a] = features(eall[1, a], False, 0.0)

    @pl.loop(0, 8)
    def _(a):
        rows = feat_l[a]
        for p in range(2):
            for b in range(8):
                tile[a, p, b] = jnp.exp2(contract(rows, feat_r[p, b], 1, 0)).astype(BF16)

    settle(recv_sem.at[1], crecv)

    @pl.loop(0, 8)
    def _(a):
        mixed = contract(tmix[...], crecv[a].reshape(256, 256), 1, 0).astype(BF16)
        pair[0, a, :256, :] = mixed
        push(3, pair.at[0, a, pl.ds(0, 256), :], pair.at[1, a, pl.ds(0, 256), :], partner)

    @pl.loop(0, 8, step=4)
    def _(a):
        for q in range(4):
            left[a + q, :, 256:] = contract(eye, pair[0, a + q, :256, :], 1, 1).astype(BF16)

    settle(recv_sem.at[3], pair.at[1, :, pl.ds(0, 256), :])

    def column(k):
        return lax.rem(x + k // 2, 4) * 2 + lax.rem(lax.rem(col, 2) + k, 2)

    def row(k):
        return lax.rem(hr // 4 + k // 4, 2) * 4 + lax.rem(y + k, 4)

    @pl.loop(0, 8)
    def _(k):
        a = column(k)
        acc = jnp.zeros((256, 256), F32)
        for p in range(2):
            for b in range(8):
                acc += contract(pair[p, b, :256, :], tile[a, p, b], 1, 1)
        osend[a] = acc.astype(BF16).reshape(8, 32, 256)

        @pl.loop(0, 8)
        def _(q):
            h = row(q)

            @pl.when(h * 8 + a != me)
            def _():
                push(4, osend.at[a, h], orecv.at[me], (a * 2 + core, h))

    keep(4, osend.at[col, hr], orecv.at[me])

    settle(recv_sem.at[2], pair.at[0, :, pl.ds(256, 256), :])
    push(5, pair.at[0, :, pl.ds(256, 256), :], pair.at[1, :, pl.ds(256, 256), :], partner)

    @pl.loop(0, 8, step=4)
    def _(a):
        for q in range(4):
            left[a + q, :, :256] = contract(eye, pair[0, a + q, 256:, :], 1, 1).astype(BF16)

    settle(recv_sem.at[5], pair.at[1, :, pl.ds(256, 256), :])

    @pl.loop(0, 8)
    def _(k):
        a = column(k)
        rows = left[a]
        for p in range(2):
            for b in range(8):
                tile[a, p, b] = contract(rows, pair[p, b], 1, 0).astype(BF16) * tile[a, p, b]
        acc = jnp.zeros((64, 256), F32)
        for p in range(2):
            for b in range(8):
                acc += contract(feat_r[p, b, :64, :], tile[a, p, b], 1, 1)
        part = acc[:16] + acc[16:32] + acc[32:48] - eall[0, a] * acc[48:49]
        esend[a] = (part * (1.0 / 16.0)).astype(BF16)

        @pl.loop(0, 8)
        def _(q):
            h = row(q)

            @pl.when(h * 8 + a != me)
            def _():
                push(6, esend.at[a], erecv.at[me], (a * 2 + core, h))

    keep(6, esend.at[col], erecv.at[me])

    settle(recv_sem.at[4], orecv)
    swap_leading(orecv, grad, perm)
    settle(recv_sem.at[6], erecv)
    egrad[...] = jnp.sum(erecv[...].astype(F32), axis=0)

    settle(send_sem.at[0], eall.at[0])
    settle(send_sem.at[0], eall.at[0, pl.ds(0, 7)])
    settle(send_sem.at[1], sent.at[pl.ds(0, 63)])
    settle(send_sem.at[2], sent.at[pl.ds(0, 63)])
    settle(send_sem.at[3], pair.at[1, :, pl.ds(0, 256), :])
    settle(send_sem.at[4], orecv.at[pl.ds(0, 63)])
    settle(send_sem.at[5], pair.at[1, :, pl.ds(256, 256), :])
    settle(send_sem.at[6], erecv.at[pl.ds(0, 63)])


def on_device(cot, field, temporal, embed):
    anywhere = pl.BlockSpec(memory_space=pl.ANY)
    vmem = pl.BlockSpec(memory_space=pltpu.VMEM)
    block = (64, 32, 256)
    return pl.pallas_call(
        kernel,
        out_shape=(
            jax.ShapeDtypeStruct((32, 64, 256), BF16),
            jax.ShapeDtypeStruct((16, 256), F32),
        ),
        in_specs=[anywhere, anywhere, vmem, vmem],
        out_specs=(vmem, vmem),
        scratch_shapes=[
            pltpu.VMEM((32, 64, 256), BF16),
            pltpu.VMEM((32, 64, 256), BF16),
            pltpu.VMEM(block, BF16),
            pltpu.VMEM(block, BF16),
            pltpu.VMEM((8, 8, 32, 256), BF16),
            pltpu.VMEM((2, 8, 512, 256), BF16),
            pltpu.VMEM((8, 2, 8, 256, 256), BF16),
            pltpu.VMEM((8, 256, 512), BF16),
            pltpu.VMEM((8, 256, 128), BF16),
            pltpu.VMEM((2, 8, 128, 256), BF16),
            pltpu.VMEM((2, 8, 16, 256), F32),
            pltpu.VMEM((256, 256), BF16),
            pltpu.VMEM((8, 8, 32, 256), BF16),
            pltpu.VMEM(block, BF16),
            pltpu.VMEM((8, 16, 256), BF16),
            pltpu.VMEM((64, 16, 256), BF16),
            pltpu.SemaphoreType.DMA((2,)),
            pltpu.SemaphoreType.DMA((7,)),
            pltpu.SemaphoreType.DMA((7,)),
        ],
        compiler_params=pltpu.CompilerParams(
            collective_id=0, has_side_effects=True, vmem_limit_bytes=50 * 2**20
        ),
    )(cot, field, temporal, embed)


def solution(mesh):
    return jax.shard_map(
        on_device,
        mesh=mesh,
        in_specs=(P("hr", None, "st"), P("hr", None, "st"), P(), P(None, "st")),
        out_specs=(P("hr", None, "st"), P(None, "st")),
        check_vma=False,
    )
```

time: 418 us -> 76.4 us (0.18)
  waiting for transfers between devices: 279 us -> 0 us
  Pallas kernels: 0 us -> 69.3 us
  blocking collectives: 63.4 us -> 0 us
  matrix products: 42.6 us -> 0 us
  between operations: 13.8 us -> 0.65 us
  local copies, waits for them, and re-layouts: 15.8 us -> 5.64 us
    all_gather x3 -> x0, waiting for transfers between devices: 221 us -> none  [the longest x1 86.3 us: on_device(): cot_piece = lax.all_gather(cotangent, 'hr', axis=0, tiled=True)]
    pallas_call x0 -> x1, Pallas kernels: none -> 69.3 us  [on_device(): pl.pallas_call(kernel, out_shape=(jax.ShapeDtypeStruct((32, 64, 256), BF1...]
    reduce_scatter x1 -> x0, waiting for transfers between devices: 56.1 us -> none  [on_device(): lax.psum_scatter(far_acc.astype(jnp.bfloat16), 'st', scatter_dimension=1,...]
    psum x1 -> x0, blocking collectives: 42.8 us -> none  [on_device(): embed_grad = lax.psum(shares, 'hr')]
    dot_general x7 -> x0, matrix products: 42.6 us -> none  [the longest x1 12.1 us: on_device(): lax.dot_general(cot_piece, ker_tile.astype(jnp.bfloat16), (((1,), (1,)),...]
    all_gather x1 -> x0, blocking collectives: 20.6 us -> none  [on_device(): lax.all_gather(embed.astype(jnp.bfloat16), 'st', axis=1, tiled=True)]
    unnamed x7 -> x10, local copies, waits for them, and re-layouts: 15.2 us -> 5.64 us
  transfers between devices with their start and end apart: 4 -> 0, of which waited for: 4 -> 0; matrix products, arithmetic and copies ran while one was open for 8% -> 0% of each run, Pallas kernels for 0% -> 0%
where the time goes in v1:
time: 76.4 us; the launch traced here: 75.6 us
  Pallas kernels  69.3 us (91%)
  local copies, waits for them, and re-layouts  5.64 us (7%)
    pallas_call x1, Pallas kernels, on_device(): pl.pallas_call(kernel, out_shape=(jax.ShapeDtypeStruct((32, 64, 256), BF1...  69.3 us
    unnamed x10, local copies, waits for them, and re-layouts  5.64 us

profile of v1, /device:TPU:0, one launch (start us, length us, event | category | flops | bytes accessed | tf_op | source)
XLA Modules:
  0.0 75.6 jit_solution(13310323356457561192)
XLA Ops:
  0.6 0.0 copy-start
  0.6 1.2 %copy-done = bf16[32,64,256]{2,1,0:T(8,128)(2,1)S(1)} copy-done((bf16[32,64,256]{2,1,0:T(8,128)(2,1)S(1)}, bf16[32,64,256]{2,1,0:T(8,128)(2,1)}, u32[]{:S(2)}) %copy-start) | copy-done | bytes 1048600
  1.9 0.0 copy-start.1
  1.9 1.2 %copy-done.1 = bf16[32,64,256]{2,1,0:T(8,128)(2,1)S(1)} copy-done((bf16[32,64,256]{2,1,0:T(8,128)(2,1)S(1)}, bf16[32,64,256]{2,1,0:T(8,128)(2,1)}, u32[]{:S(2)}) %copy-start.1) | copy-done | bytes 1048600
  3.1 0.0 copy-start.2
  3.1 0.9 %copy-done.2 = bf16[256,256]{1,0:T(8,128)(2,1)S(1)} copy-done((bf16[256,256]{1,0:T(8,128)(2,1)S(1)}, bf16[256,256]{1,0:T(8,128)(2,1)}, u32[]{:S(2)}) %copy-start.2) | copy-done | bytes 131096
  4.0 0.0 copy-start.3
  4.0 0.7 copy-done.3
  4.7 69.3 %shard_map.59 = (bf16[32,64,256]{2,1,0:T(8,128)(2,1)S(1)}, f32[16,256]{1,0:T(8,128)S(1)}) custom-call(bf16[32,64,256]{2,1,0:T(8,128)(2,1)S(1)} %copy-done, bf16[32,64,256]{2,1,0:T(8,128)(2,1)S(1)} %copy-done.1, bf16[256,256]{1,0:T(8,128)(2,1)S(1)} %copy-done.2, f32[16,256]{1,0:T(8,128)S(1)} %copy-done.3), custom_call_target="tpu_custom_call" | custom-call | tf_op jit(solution)/shard_map/pallas_call | solution.py:270
  74.0 1.0 %copy.8 = bf16[32,64,256]{2,1,0:T(8,128)(2,1)} copy(bf16[32,64,256]{2,1,0:T(8,128)(2,1)S(1)} %get-tuple-element.4) | data formatting | bytes 2097152
  75.0 0.6 copy.9
Async XLA Ops:
  0.6 1.2 %copy-start = (bf16[32,64,256]{2,1,0:T(8,128)(2,1)S(1)}, bf16[32,64,256]{2,1,0:T(8,128)(2,1)}, u32[]{:S(2)}) copy-start(bf16[32,64,256]{2,1,0:T(8,128)(2,1)} %cot.1) | copy-start | bytes 3145732
  1.9 1.2 %copy-start.1 = (bf16[32,64,256]{2,1,0:T(8,128)(2,1)S(1)}, bf16[32,64,256]{2,1,0:T(8,128)(2,1)}, u32[]{:S(2)}) copy-start(bf16[32,64,256]{2,1,0:T(8,128)(2,1)} %field.1) | copy-start | bytes 3145732
  3.1 0.9 %copy-start.2 = (bf16[256,256]{1,0:T(8,128)(2,1)S(1)}, bf16[256,256]{1,0:T(8,128)(2,1)}, u32[]{:S(2)}) copy-start(bf16[256,256]{1,0:T(8,128)(2,1)} %temporal.1) | copy-start | bytes 393220
  4.0 0.7 copy-start.3

commit v2 on v1

--- a/solution.py
+++ b/solution.py
@@ -68,13 +68,13 @@
     else:
         h, m, l = split3(e)
         rows = [h, m, l, norm_rows(sq, False, 0.0), h, m, h, zero]
-    return jnp.concatenate([r.astype(F32) for r in rows], axis=0).astype(BF16)
+    return jnp.concatenate(rows, axis=0)
 
 
 def kernel(
-    cot, field, temporal, embed, grad, egrad,
-    raw, fraw, sent, fsent, crecv, pair, tile, left, feat_l, feat_r,
-    eall, tmix, osend, orecv, esend, erecv,
+    cot, field, temporal_in, embed_in, grad, egrad,
+    raw, fraw, temporal, embed, sent, fsent, crecv, pair, tile, left, feat_l, feat_r,
+    eall, tmix, osend, orecv, esend, erecv, gsend, grecv,
     in_sem, send_sem, recv_sem,
 ):
     st = lax.axis_index("st")
@@ -86,15 +86,18 @@
     partner = (st + 1 - 2 * core, hr)
 
     def peer(k):
-        px = lax.rem(x + lax.rem(k, 4), 4)
-        py = lax.rem(y + lax.rem(k // 4, 4), 4)
-        pz = lax.rem(z + k // 16, 4)
+        step = lax.rem(k, 4)
+        px = lax.rem(x + step, 4)
+        py = lax.rem(y + k // 4 + step, 4)
+        pz = lax.rem(z + k // 16 + step, 4)
         return px * 2 + lax.rem(pz, 2), (pz // 2) * 4 + py
 
     def load(i, src, dst):
         return pltpu.make_async_copy(src, dst, in_sem.at[i])
 
+    load(2, embed_in, embed).start()
     load(0, cot, raw).start()
+    load(3, temporal_in, temporal).start()
     load(1, field, fraw).start()
 
     barrier = pltpu.get_barrier_semaphore()
@@ -111,6 +114,7 @@
     perm = swap_rows()
     load(0, cot, raw).wait()
     swap_leading(raw, sent, perm)
+    load(2, embed_in, embed).wait()
     pl.semaphore_wait(barrier, 71)
 
     def push(i, src, dst, device):
@@ -148,44 +152,55 @@
     swap_leading(fraw, fsent, perm)
     hours = pl.ds(pl.multiple_of(256 + hr * 32, 32), 32)
 
-    @pl.loop(1, 64)
-    def _(k):
+    def push_field(k):
         c, h = peer(k)
         push(2, fsent.at[h * 8 + c], pair.at[0, col, hours, :], (c * 2 + core, h))
 
-    keep(2, fsent.at[me], pair.at[0, col, hours, :])
-
     eye = identity()
+    load(3, temporal_in, temporal).wait()
     tmix[...] = contract(eye, temporal[...], 1, 1).astype(BF16)
     amp_log2 = -0.5 * math.log2(4096.0)
     settle(recv_sem.at[0], eall)
 
-    @pl.loop(0, 8)
-    def _(a):
-        e = eall[0, a]
-        feat_l[a] = contract(eye, features(e, True, amp_log2), 1, 1).astype(BF16)
-        feat_r[0, a] = features(e, False, 0.0)
-        feat_r[1, a] = features(eall[1, a], False, 0.0)
-
-    @pl.loop(0, 8)
-    def _(a):
+    @pl.loop(0, 8, step=2)
+    def _(a):
+        for q in range(2):
+            e = eall[0, a + q]
+            feat_l[a + q] = contract(eye, features(e, True, amp_log2), 1, 1).astype(BF16)
+            feat_r[0, a + q] = features(e, False, 0.0)
+            feat_r[1, a + q] = features(eall[1, a + q], False, 0.0)
+
+    def station_tiles(a, p):
         rows = feat_l[a]
-        for p in range(2):
-            for b in range(8):
-                tile[a, p, b] = jnp.exp2(contract(rows, feat_r[p, b], 1, 0)).astype(BF16)
+        for b in range(8):
+            tile[a, p, b] = jnp.exp2(contract(rows, feat_r[p, b], 1, 0)).astype(BF16)
+
+    @pl.loop(0, 8)
+    def _(a):
+        @pl.when(a > 0)
+        def _():
+            push_field(a * 8)
+
+        for q in range(1, 8):
+            push_field(a * 8 + q)
+        station_tiles(a, 0)
+
+    keep(2, fsent.at[me], pair.at[0, col, hours, :])
 
     settle(recv_sem.at[1], crecv)
 
-    @pl.loop(0, 8)
-    def _(a):
-        mixed = contract(tmix[...], crecv[a].reshape(256, 256), 1, 0).astype(BF16)
-        pair[0, a, :256, :] = mixed
-        push(3, pair.at[0, a, pl.ds(0, 256), :], pair.at[1, a, pl.ds(0, 256), :], partner)
-
-    @pl.loop(0, 8, step=4)
-    def _(a):
-        for q in range(4):
-            left[a + q, :, 256:] = contract(eye, pair[0, a + q, :256, :], 1, 1).astype(BF16)
+    @pl.loop(0, 8, step=2)
+    def _(a):
+        for q in range(2):
+            mixed = contract(tmix[...], crecv[a + q].reshape(256, 256), 1, 0).astype(BF16)
+            pair[0, a + q, :256, :] = mixed
+        both = pl.ds(a, 2)
+        push(3, pair.at[0, both, pl.ds(0, 256), :], pair.at[1, both, pl.ds(0, 256), :], partner)
+
+    @pl.loop(0, 8)
+    def _(a):
+        left[a, :, 256:] = contract(eye, pair[0, a, :256, :], 1, 1).astype(BF16)
+        station_tiles(a, 1)
 
     settle(recv_sem.at[3], pair.at[1, :, pl.ds(0, 256), :])
 
@@ -195,23 +210,26 @@
     def row(k):
         return lax.rem(hr // 4 + k // 4, 2) * 4 + lax.rem(y + k, 4)
 
-    @pl.loop(0, 8)
-    def _(k):
-        a = column(k)
+    def grad_block(a):
         acc = jnp.zeros((256, 256), F32)
         for p in range(2):
             for b in range(8):
                 acc += contract(pair[p, b, :256, :], tile[a, p, b], 1, 1)
         osend[a] = acc.astype(BF16).reshape(8, 32, 256)
 
-        @pl.loop(0, 8)
-        def _(q):
+    def push_grad(a, first):
+        for q in range(first, 8):
             h = row(q)
-
-            @pl.when(h * 8 + a != me)
-            def _():
-                push(4, osend.at[a, h], orecv.at[me], (a * 2 + core, h))
-
+            push(4, osend.at[a, h], orecv.at[me], (a * 2 + core, h))
+
+    @pl.loop(1, 8)
+    def _(k):
+        a = column(k)
+        grad_block(a)
+        push_grad(a, 0)
+
+    grad_block(col)
+    push_grad(col, 1)
     keep(4, osend.at[col, hr], orecv.at[me])
 
     settle(recv_sem.at[2], pair.at[0, :, pl.ds(256, 256), :])
@@ -222,36 +240,65 @@
         for q in range(4):
             left[a + q, :, :256] = contract(eye, pair[0, a + q, 256:, :], 1, 1).astype(BF16)
 
+    @pl.loop(0, 8)
+    def _(a):
+        rows = left[a]
+        for d in range(5):
+            b = lax.rem(a + d, 8)
+            tile[a, 0, b] = contract(rows, pair[0, b], 1, 0).astype(BF16) * tile[a, 0, b]
+
     settle(recv_sem.at[5], pair.at[1, :, pl.ds(256, 256), :])
 
     @pl.loop(0, 8)
-    def _(k):
-        a = column(k)
+    def _(a):
         rows = left[a]
-        for p in range(2):
-            for b in range(8):
-                tile[a, p, b] = contract(rows, pair[p, b], 1, 0).astype(BF16) * tile[a, p, b]
+        for d in range(4):
+            b = lax.rem(a + core + d, 8)
+            tile[a, 1, b] = contract(rows, pair[1, b], 1, 0).astype(BF16) * tile[a, 1, b]
+
+    def fold(acc, e):
+        return acc[:16] + acc[16:32] + acc[32:48] - e * acc[48:49]
+
+    @pl.loop(1, 9)
+    def _(k):
+        b = lax.rem(col + k, 8)
         acc = jnp.zeros((64, 256), F32)
-        for p in range(2):
-            for b in range(8):
-                acc += contract(feat_r[p, b, :64, :], tile[a, p, b], 1, 1)
-        part = acc[:16] + acc[16:32] + acc[32:48] - eall[0, a] * acc[48:49]
-        esend[a] = (part * (1.0 / 16.0)).astype(BF16)
-
-        @pl.loop(0, 8)
-        def _(q):
-            h = row(q)
-
-            @pl.when(h * 8 + a != me)
-            def _():
-                push(6, esend.at[a], erecv.at[me], (a * 2 + core, h))
-
-    keep(6, esend.at[col], erecv.at[me])
+        for d in range(4):
+            a = lax.rem(b + 16 - core - d, 8)
+            acc += contract(feat_r[0, a, :64, :], tile[a, 1, b], 1, 0)
+        esend[1, b] = fold(acc, eall[1, b]).astype(BF16)
+        push(6, esend.at[1, b], erecv.at[st], (b * 2 + 1 - core, hr))
+
+    @pl.loop(1, 9)
+    def _(k):
+        a = lax.rem(col + k, 8)
+        acc = jnp.zeros((64, 256), F32)
+        for d in range(5):
+            b = lax.rem(a + d, 8)
+            acc += contract(feat_r[0, b, :64, :], tile[a, 0, b], 1, 1)
+        for d in range(4):
+            b = lax.rem(a + core + d, 8)
+            acc += contract(feat_r[1, b, :64, :], tile[a, 1, b], 1, 1)
+        for d in range(1, 4):
+            b = lax.rem(a + 8 - d, 8)
+            acc += contract(feat_r[0, b, :64, :], tile[b, 0, a], 1, 0)
+        esend[0, a] = fold(acc, eall[0, a]).astype(BF16)
+
+        @pl.when(k < 8)
+        def _():
+            push(6, esend.at[0, a], erecv.at[st], (a * 2 + core, hr))
+
+    erecv[st] = esend[0, col]
+    settle(recv_sem.at[6], erecv.at[pl.ds(0, 15)])
+    gsend[...] = jnp.sum(erecv[...].astype(F32), axis=0) * (1.0 / 16.0)
+    for k in range(1, 8):
+        push(7, gsend, grecv.at[hr], (st, lax.rem(hr + k, 8)))
+    grecv[hr] = gsend[...]
 
     settle(recv_sem.at[4], orecv)
     swap_leading(orecv, grad, perm)
-    settle(recv_sem.at[6], erecv)
-    egrad[...] = jnp.sum(erecv[...].astype(F32), axis=0)
+    settle(recv_sem.at[7], grecv.at[pl.ds(0, 7)])
+    egrad[...] = jnp.sum(grecv[...], axis=0)
 
     settle(send_sem.at[0], eall.at[0])
     settle(send_sem.at[0], eall.at[0, pl.ds(0, 7)])
@@ -260,11 +307,12 @@
     settle(send_sem.at[3], pair.at[1, :, pl.ds(0, 256), :])
     settle(send_sem.at[4], orecv.at[pl.ds(0, 63)])
     settle(send_sem.at[5], pair.at[1, :, pl.ds(256, 256), :])
-    settle(send_sem.at[6], erecv.at[pl.ds(0, 63)])
+    settle(send_sem.at[6], erecv.at[pl.ds(0, 15)])
+    settle(send_sem.at[7], grecv.at[pl.ds(0, 7)])
 
 
 def on_device(cot, field, temporal, embed):
-    anywhere = pl.BlockSpec(memory_space=pl.ANY)
+    hbm = pl.BlockSpec(memory_space=pltpu.HBM)
     vmem = pl.BlockSpec(memory_space=pltpu.VMEM)
     block = (64, 32, 256)
     return pl.pallas_call(
@@ -273,11 +321,13 @@
             jax.ShapeDtypeStruct((32, 64, 256), BF16),
             jax.ShapeDtypeStruct((16, 256), F32),
         ),
-        in_specs=[anywhere, anywhere, vmem, vmem],
+        in_specs=[hbm, hbm, hbm, hbm],
         out_specs=(vmem, vmem),
         scratch_shapes=[
             pltpu.VMEM((32, 64, 256), BF16),
             pltpu.VMEM((32, 64, 256), BF16),
+            pltpu.VMEM((256, 256), BF16),
+            pltpu.VMEM((16, 256), F32),
             pltpu.VMEM(block, BF16),
             pltpu.VMEM(block, BF16),
             pltpu.VMEM((8, 8, 32, 256), BF16),
@@ -290,14 +340,16 @@
             pltpu.VMEM((256, 256), BF16),
             pltpu.VMEM((8, 8, 32, 256), BF16),
             pltpu.VMEM(block, BF16),
-            pltpu.VMEM((8, 16, 256), BF16),
-            pltpu.VMEM((64, 16, 256), BF16),
-            pltpu.SemaphoreType.DMA((2,)),
-            pltpu.SemaphoreType.DMA((7,)),
-            pltpu.SemaphoreType.DMA((7,)),
+            pltpu.VMEM((2, 8, 16, 256), BF16),
+            pltpu.VMEM((16, 16, 256), BF16),
+            pltpu.VMEM((16, 256), F32),
+            pltpu.VMEM((8, 16, 256), F32),
+            pltpu.SemaphoreType.DMA((4,)),
+            pltpu.SemaphoreType.DMA((8,)),
+            pltpu.SemaphoreType.DMA((8,)),
         ],
         compiler_params=pltpu.CompilerParams(
-            collective_id=0, has_side_effects=True, vmem_limit_bytes=50 * 2**20
+            collective_id=0, has_side_effects=True, vmem_limit_bytes=52 * 2**20
         ),
     )(cot, field, temporal, embed)
 

time: 76.4 us -> 69.1 us (0.904)
  Pallas kernels: 69.3 us -> 65.1 us
  local copies, waits for them, and re-layouts: 5.64 us -> 3.19 us
    pallas_call x1, Pallas kernels: 69.3 us -> 65.1 us  [on_device(): pl.pallas_call(kernel, out_shape=(jax.ShapeDtypeStruct((32, 64, 256), BF1...]
    unnamed x10 -> x6, local copies, waits for them, and re-layouts: 5.64 us -> 3.19 us
where the time goes in v2:
time: 69.1 us; the launch traced here: 69 us
  Pallas kernels  65.1 us (94%)
  local copies, waits for them, and re-layouts  3.19 us (5%)
    pallas_call x1, Pallas kernels, on_device(): pl.pallas_call(kernel, out_shape=(jax.ShapeDtypeStruct((32, 64, 256), BF1...  65.1 us
    unnamed x6, local copies, waits for them, and re-layouts  3.19 us

profile of v2, /device:TPU:0, one launch (start us, length us, event | category | flops | bytes accessed | tf_op | source)
XLA Modules:
  0.0 69.0 jit_solution(7559998232807440676)
XLA Ops:
  0.6 0.0 copy-start
  0.6 0.9 %copy-done = bf16[256,256]{1,0:T(8,128)(2,1)S(1)} copy-done((bf16[256,256]{1,0:T(8,128)(2,1)S(1)}, bf16[256,256]{1,0:T(8,128)(2,1)}, u32[]{:S(2)}) %copy-start) | copy-done | bytes 131096
  1.5 0.0 copy-start.1
  1.5 0.7 %copy-done.1 = f32[16,256]{1,0:T(8,128)S(1)} copy-done((f32[16,256]{1,0:T(8,128)S(1)}, f32[16,256]{1,0:T(8,128)}, u32[]{:S(2)}) %copy-start.1) | copy-done | bytes 16408
  2.3 65.1 %shard_map.59 = (bf16[32,64,256]{2,1,0:T(8,128)(2,1)S(1)}, f32[16,256]{1,0:T(8,128)S(1)}) custom-call(bf16[32,64,256]{2,1,0:T(8,128)(2,1)} %cot.1, bf16[32,64,256]{2,1,0:T(8,128)(2,1)} %field.1, bf16[256,256]{1,0:T(8,128)(2,1)S(1)} %copy-done, f32[16,256]{1,0:T(8,128)S(1)} %copy-done.1), custom_call_target="tpu_custom_call" | custom-call | tf_op jit(solution)/shard_map/pallas_call | solution.py:318
  67.4 1.0 %copy.8 = bf16[32,64,256]{2,1,0:T(8,128)(2,1)} copy(bf16[32,64,256]{2,1,0:T(8,128)(2,1)S(1)} %get-tuple-element.4) | data formatting | bytes 2097152
  68.4 0.6 copy.9
Async XLA Ops:
  0.6 0.9 %copy-start = (bf16[256,256]{1,0:T(8,128)(2,1)S(1)}, bf16[256,256]{1,0:T(8,128)(2,1)}, u32[]{:S(2)}) copy-start(bf16[256,256]{1,0:T(8,128)(2,1)} %temporal_in.1) | copy-start | bytes 393220
  1.5 0.7 %copy-start.1 = (f32[16,256]{1,0:T(8,128)S(1)}, f32[16,256]{1,0:T(8,128)}, u32[]{:S(2)}) copy-start(f32[16,256]{1,0:T(8,128)} %embed_in.1) | copy-start | bytes 49156

commit v3 on v2

--- a/solution.py
+++ b/solution.py
@@ -74,7 +74,7 @@
 def kernel(
     cot, field, temporal_in, embed_in, grad, egrad,
     raw, fraw, temporal, embed, sent, fsent, crecv, pair, tile, left, feat_l, feat_r,
-    eall, tmix, osend, orecv, esend, erecv, gsend, grecv,
+    eall, tmix, osend, orecv, esend, erecv, gsend, grecv, inner, cross,
     in_sem, send_sem, recv_sem,
 ):
     st = lax.axis_index("st")
@@ -184,6 +184,7 @@
         for q in range(1, 8):
             push_field(a * 8 + q)
         station_tiles(a, 0)
+        station_tiles(a, 1)
 
     keep(2, fsent.at[me], pair.at[0, col, hours, :])
 
@@ -200,7 +201,6 @@
     @pl.loop(0, 8)
     def _(a):
         left[a, :, 256:] = contract(eye, pair[0, a, :256, :], 1, 1).astype(BF16)
-        station_tiles(a, 1)
 
     settle(recv_sem.at[3], pair.at[1, :, pl.ds(0, 256), :])
 
@@ -222,13 +222,16 @@
             h = row(q)
             push(4, osend.at[a, h], orecv.at[me], (a * 2 + core, h))
 
-    @pl.loop(1, 8)
-    def _(k):
-        a = column(k)
-        grad_block(a)
-        push_grad(a, 0)
-
+    @pl.loop(1, 7, step=2)
+    def _(k):
+        grad_block(column(k))
+        grad_block(column(k + 1))
+        push_grad(column(k), 0)
+        push_grad(column(k + 1), 0)
+
+    grad_block(column(7))
     grad_block(col)
+    push_grad(column(7), 0)
     push_grad(col, 1)
     keep(4, osend.at[col, hr], orecv.at[me])
 
@@ -240,53 +243,69 @@
         for q in range(4):
             left[a + q, :, :256] = contract(eye, pair[0, a + q, 256:, :], 1, 1).astype(BF16)
 
-    @pl.loop(0, 8)
-    def _(a):
-        rows = left[a]
-        for d in range(5):
-            b = lax.rem(a + d, 8)
-            tile[a, 0, b] = contract(rows, pair[0, b], 1, 0).astype(BF16) * tile[a, 0, b]
+    @pl.loop(0, 8, step=4)
+    def _(first):
+        for q in range(4):
+            a = first + q
+            rows = left[a]
+            for d in range(5):
+                b = lax.rem(a + d, 8)
+                gram = contract(rows, pair[0, b], 1, 0).astype(BF16)
+                inner[a, d] = gram * tile[a, 0, b]
 
     settle(recv_sem.at[5], pair.at[1, :, pl.ds(256, 256), :])
 
-    @pl.loop(0, 8)
-    def _(a):
-        rows = left[a]
-        for d in range(4):
-            b = lax.rem(a + core + d, 8)
-            tile[a, 1, b] = contract(rows, pair[1, b], 1, 0).astype(BF16) * tile[a, 1, b]
+    @pl.loop(0, 8, step=4)
+    def _(first):
+        for q in range(4):
+            a = first + q
+            rows = left[a]
+            for d in range(4):
+                b = lax.rem(a + core + d, 8)
+                gram = contract(rows, pair[1, b], 1, 0).astype(BF16)
+                cross[a, d] = gram * tile[a, 1, b]
 
     def fold(acc, e):
         return acc[:16] + acc[16:32] + acc[32:48] - e * acc[48:49]
 
-    @pl.loop(1, 9)
-    def _(k):
-        b = lax.rem(col + k, 8)
+    def other_part(b):
         acc = jnp.zeros((64, 256), F32)
         for d in range(4):
             a = lax.rem(b + 16 - core - d, 8)
-            acc += contract(feat_r[0, a, :64, :], tile[a, 1, b], 1, 0)
-        esend[1, b] = fold(acc, eall[1, b]).astype(BF16)
-        push(6, esend.at[1, b], erecv.at[st], (b * 2 + 1 - core, hr))
-
-    @pl.loop(1, 9)
-    def _(k):
-        a = lax.rem(col + k, 8)
+            acc += contract(feat_r[0, a, :64, :], cross[a, d], 1, 0)
+        return fold(acc, eall[1, b]).astype(BF16)
+
+    def own_part(a):
         acc = jnp.zeros((64, 256), F32)
         for d in range(5):
-            b = lax.rem(a + d, 8)
-            acc += contract(feat_r[0, b, :64, :], tile[a, 0, b], 1, 1)
+            acc += contract(feat_r[0, lax.rem(a + d, 8), :64, :], inner[a, d], 1, 1)
         for d in range(4):
-            b = lax.rem(a + core + d, 8)
-            acc += contract(feat_r[1, b, :64, :], tile[a, 1, b], 1, 1)
+            acc += contract(feat_r[1, lax.rem(a + core + d, 8), :64, :], cross[a, d], 1, 1)
         for d in range(1, 4):
             b = lax.rem(a + 8 - d, 8)
-            acc += contract(feat_r[0, b, :64, :], tile[b, 0, a], 1, 0)
-        esend[0, a] = fold(acc, eall[0, a]).astype(BF16)
-
-        @pl.when(k < 8)
-        def _():
-            push(6, esend.at[0, a], erecv.at[st], (a * 2 + core, hr))
+            acc += contract(feat_r[0, b, :64, :], inner[b, d], 1, 0)
+        return fold(acc, eall[0, a]).astype(BF16)
+
+    @pl.loop(1, 9, step=2)
+    def _(k):
+        for q in range(2):
+            b = lax.rem(col + k + q, 8)
+            esend[1, b] = other_part(b)
+        for q in range(2):
+            b = lax.rem(col + k + q, 8)
+            push(6, esend.at[1, b], erecv.at[st], (b * 2 + 1 - core, hr))
+
+    @pl.loop(1, 9, step=2)
+    def _(k):
+        for q in range(2):
+            a = lax.rem(col + k + q, 8)
+            esend[0, a] = own_part(a)
+        for q in range(2):
+            a = lax.rem(col + k + q, 8)
+
+            @pl.when(k + q < 8)
+            def _():
+                push(6, esend.at[0, a], erecv.at[st], (a * 2 + core, hr))
 
     erecv[st] = esend[0, col]
     settle(recv_sem.at[6], erecv.at[pl.ds(0, 15)])
@@ -344,6 +363,8 @@
             pltpu.VMEM((16, 16, 256), BF16),
             pltpu.VMEM((16, 256), F32),
             pltpu.VMEM((8, 16, 256), F32),
+            pltpu.VMEM((8, 5, 256, 256), BF16),
+            pltpu.VMEM((8, 4, 256, 256), BF16),
             pltpu.SemaphoreType.DMA((4,)),
             pltpu.SemaphoreType.DMA((8,)),
             pltpu.SemaphoreType.DMA((8,)),

time: 69.1 us -> 65.4 us (0.946)
  Pallas kernels: 65.1 us -> 61.4 us
    pallas_call x1, Pallas kernels: 65.1 us -> 61.4 us  [on_device(): pl.pallas_call(kernel, out_shape=(jax.ShapeDtypeStruct((32, 64, 256), BF1...]
where the time goes in v3:
time: 65.4 us; the launch traced here: 65.3 us
  Pallas kernels  61.4 us (94%)
  local copies, waits for them, and re-layouts  3.19 us (5%)
    pallas_call x1, Pallas kernels, on_device(): pl.pallas_call(kernel, out_shape=(jax.ShapeDtypeStruct((32, 64, 256), BF1...  61.4 us
    unnamed x6, local copies, waits for them, and re-layouts  3.19 us

profile of v3, /device:TPU:0, one launch (start us, length us, event | category | flops | bytes accessed | tf_op | source)
XLA Modules:
  0.0 65.3 jit_solution(17129344491992777470)
XLA Ops:
  0.6 0.0 copy-start
  0.6 0.9 %copy-done = bf16[256,256]{1,0:T(8,128)(2,1)S(1)} copy-done((bf16[256,256]{1,0:T(8,128)(2,1)S(1)}, bf16[256,256]{1,0:T(8,128)(2,1)}, u32[]{:S(2)}) %copy-start) | copy-done | bytes 131096
  1.5 0.0 copy-start.1
  1.5 0.7 %copy-done.1 = f32[16,256]{1,0:T(8,128)S(1)} copy-done((f32[16,256]{1,0:T(8,128)S(1)}, f32[16,256]{1,0:T(8,128)}, u32[]{:S(2)}) %copy-start.1) | copy-done | bytes 16408
  2.3 61.4 %shard_map.59 = (bf16[32,64,256]{2,1,0:T(8,128)(2,1)S(1)}, f32[16,256]{1,0:T(8,128)S(1)}) custom-call(bf16[32,64,256]{2,1,0:T(8,128)(2,1)} %cot.1, bf16[32,64,256]{2,1,0:T(8,128)(2,1)} %field.1, bf16[256,256]{1,0:T(8,128)(2,1)S(1)} %copy-done, f32[16,256]{1,0:T(8,128)S(1)} %copy-done.1), custom_call_target="tpu_custom_call" | custom-call | tf_op jit(solution)/shard_map/pallas_call | solution.py:337
  63.7 1.0 %copy.8 = bf16[32,64,256]{2,1,0:T(8,128)(2,1)} copy(bf16[32,64,256]{2,1,0:T(8,128)(2,1)S(1)} %get-tuple-element.4) | data formatting | bytes 2097152
  64.7 0.6 copy.9
Async XLA Ops:
  0.6 0.9 %copy-start = (bf16[256,256]{1,0:T(8,128)(2,1)S(1)}, bf16[256,256]{1,0:T(8,128)(2,1)}, u32[]{:S(2)}) copy-start(bf16[256,256]{1,0:T(8,128)(2,1)} %temporal_in.1) | copy-start | bytes 393220
  1.5 0.7 %copy-start.1 = (f32[16,256]{1,0:T(8,128)S(1)}, f32[16,256]{1,0:T(8,128)}, u32[]{:S(2)}) copy-start(f32[16,256]{1,0:T(8,128)} %embed_in.1) | copy-start | bytes 49156

commit v4 on v3

--- a/solution.py
+++ b/solution.py
@@ -134,11 +134,6 @@
         c = lax.rem(col + k, 8)
         push(0, embed, eall.at[0, col], (c * 2 + core, hr))
 
-    @pl.loop(0, 8)
-    def _(k):
-        c = lax.rem(col + k, 8)
-        push(0, embed, eall.at[1, col], (c * 2 + 1 - core, hr))
-
     keep(0, embed, eall.at[0, col])
 
     @pl.loop(1, 64)
@@ -160,7 +155,8 @@
     load(3, temporal_in, temporal).wait()
     tmix[...] = contract(eye, temporal[...], 1, 1).astype(BF16)
     amp_log2 = -0.5 * math.log2(4096.0)
-    settle(recv_sem.at[0], eall)
+    settle(recv_sem.at[0], eall.at[0])
+    push(8, eall.at[0], eall.at[1], partner)
 
     @pl.loop(0, 8, step=2)
     def _(a):
@@ -168,7 +164,6 @@
             e = eall[0, a + q]
             feat_l[a + q] = contract(eye, features(e, True, amp_log2), 1, 1).astype(BF16)
             feat_r[0, a + q] = features(e, False, 0.0)
-            feat_r[1, a + q] = features(eall[1, a + q], False, 0.0)
 
     def station_tiles(a, p):
         rows = feat_l[a]
@@ -179,11 +174,23 @@
     def _(a):
         @pl.when(a > 0)
         def _():
-            push_field(a * 8)
-
-        for q in range(1, 8):
-            push_field(a * 8 + q)
+            push_field(a * 4)
+
+        for q in range(1, 4):
+            push_field(a * 4 + q)
         station_tiles(a, 0)
+
+    settle(recv_sem.at[8], eall.at[1])
+
+    @pl.loop(0, 8, step=2)
+    def _(a):
+        for q in range(2):
+            feat_r[1, a + q] = features(eall[1, a + q], False, 0.0)
+
+    @pl.loop(0, 8)
+    def _(a):
+        for q in range(4):
+            push_field(32 + a * 4 + q)
         station_tiles(a, 1)
 
     keep(2, fsent.at[me], pair.at[0, col, hours, :])
@@ -239,14 +246,10 @@
     push(5, pair.at[0, :, pl.ds(256, 256), :], pair.at[1, :, pl.ds(256, 256), :], partner)
 
     @pl.loop(0, 8, step=4)
-    def _(a):
-        for q in range(4):
-            left[a + q, :, :256] = contract(eye, pair[0, a + q, 256:, :], 1, 1).astype(BF16)
-
-    @pl.loop(0, 8, step=4)
     def _(first):
         for q in range(4):
             a = first + q
+            left[a, :, :256] = pair[0, a, 256:, :].T
             rows = left[a]
             for d in range(5):
                 b = lax.rem(a + d, 8)
@@ -319,8 +322,8 @@
     settle(recv_sem.at[7], grecv.at[pl.ds(0, 7)])
     egrad[...] = jnp.sum(grecv[...], axis=0)
 
-    settle(send_sem.at[0], eall.at[0])
     settle(send_sem.at[0], eall.at[0, pl.ds(0, 7)])
+    settle(send_sem.at[8], eall.at[1])
     settle(send_sem.at[1], sent.at[pl.ds(0, 63)])
     settle(send_sem.at[2], sent.at[pl.ds(0, 63)])
     settle(send_sem.at[3], pair.at[1, :, pl.ds(0, 256), :])
@@ -366,8 +369,8 @@
             pltpu.VMEM((8, 5, 256, 256), BF16),
             pltpu.VMEM((8, 4, 256, 256), BF16),
             pltpu.SemaphoreType.DMA((4,)),
-            pltpu.SemaphoreType.DMA((8,)),
-            pltpu.SemaphoreType.DMA((8,)),
+            pltpu.SemaphoreType.DMA((9,)),
+            pltpu.SemaphoreType.DMA((9,)),
         ],
         compiler_params=pltpu.CompilerParams(
             collective_id=0, has_side_effects=True, vmem_limit_bytes=52 * 2**20

time: 65.4 us -> 63.6 us (0.972)
  Pallas kernels: 61.4 us -> 59.4 us
    pallas_call x1, Pallas kernels: 61.4 us -> 59.4 us  [on_device(): pl.pallas_call(kernel, out_shape=(jax.ShapeDtypeStruct((32, 64, 256), BF1...]
where the time goes in v4:
time: 63.6 us; the launch traced here: 63.2 us
  Pallas kernels  59.4 us (93%)
  local copies, waits for them, and re-layouts  3.19 us (5%)
  between operations  0.65 us (1%)
    pallas_call x1, Pallas kernels, on_device(): pl.pallas_call(kernel, out_shape=(jax.ShapeDtypeStruct((32, 64, 256), BF1...  59.4 us
    unnamed x6, local copies, waits for them, and re-layouts  3.19 us

profile of v4, /device:TPU:0, one launch (start us, length us, event | category | flops | bytes accessed | tf_op | source)
XLA Modules:
  0.0 63.2 jit_solution(10858229739528921392)
XLA Ops:
  0.6 0.0 copy-start
  0.6 0.9 %copy-done = bf16[256,256]{1,0:T(8,128)(2,1)S(1)} copy-done((bf16[256,256]{1,0:T(8,128)(2,1)S(1)}, bf16[256,256]{1,0:T(8,128)(2,1)}, u32[]{:S(2)}) %copy-start) | copy-done | bytes 131096
  1.5 0.0 copy-start.1
  1.5 0.7 %copy-done.1 = f32[16,256]{1,0:T(8,128)S(1)} copy-done((f32[16,256]{1,0:T(8,128)S(1)}, f32[16,256]{1,0:T(8,128)}, u32[]{:S(2)}) %copy-start.1) | copy-done | bytes 16408
  2.3 59.4 %shard_map.59 = (bf16[32,64,256]{2,1,0:T(8,128)(2,1)S(1)}, f32[16,256]{1,0:T(8,128)S(1)}) custom-call(bf16[32,64,256]{2,1,0:T(8,128)(2,1)} %cot.1, bf16[32,64,256]{2,1,0:T(8,128)(2,1)} %field.1, bf16[256,256]{1,0:T(8,128)(2,1)S(1)} %copy-done, f32[16,256]{1,0:T(8,128)S(1)} %copy-done.1), custom_call_target="tpu_custom_call" | custom-call | tf_op jit(solution)/shard_map/pallas_call | solution.py:340
  61.7 1.0 %copy.8 = bf16[32,64,256]{2,1,0:T(8,128)(2,1)} copy(bf16[32,64,256]{2,1,0:T(8,128)(2,1)S(1)} %get-tuple-element.4) | data formatting | bytes 2097152
  62.6 0.6 copy.9
Async XLA Ops:
  0.6 0.9 %copy-start = (bf16[256,256]{1,0:T(8,128)(2,1)S(1)}, bf16[256,256]{1,0:T(8,128)(2,1)}, u32[]{:S(2)}) copy-start(bf16[256,256]{1,0:T(8,128)(2,1)} %temporal_in.1) | copy-start | bytes 393220
  1.5 0.7 %copy-start.1 = (f32[16,256]{1,0:T(8,128)S(1)}, f32[16,256]{1,0:T(8,128)}, u32[]{:S(2)}) copy-start(f32[16,256]{1,0:T(8,128)} %embed_in.1) | copy-start | bytes 49156

commit v5 on v4

--- a/solution.py
+++ b/solution.py
@@ -212,7 +212,7 @@
     settle(recv_sem.at[3], pair.at[1, :, pl.ds(0, 256), :])
 
     def column(k):
-        return lax.rem(x + k // 2, 4) * 2 + lax.rem(lax.rem(col, 2) + k, 2)
+        return lax.rem(x + lax.rem(k, 4), 4) * 2 + lax.rem(lax.rem(col, 2) + k // 4, 2)
 
     def row(k):
         return lax.rem(hr // 4 + k // 4, 2) * 4 + lax.rem(y + k, 4)
@@ -289,12 +289,12 @@
             acc += contract(feat_r[0, b, :64, :], inner[b, d], 1, 0)
         return fold(acc, eall[0, a]).astype(BF16)
 
-    @pl.loop(1, 9, step=2)
-    def _(k):
-        for q in range(2):
+    @pl.loop(1, 9, step=4)
+    def _(k):
+        for q in range(4):
             b = lax.rem(col + k + q, 8)
             esend[1, b] = other_part(b)
-        for q in range(2):
+        for q in range(4):
             b = lax.rem(col + k + q, 8)
             push(6, esend.at[1, b], erecv.at[st], (b * 2 + 1 - core, hr))
 

time: 63.6 us -> 63.4 us (level)
  no operation moved by 1% of the time
where the time goes in v5:
time: 63.4 us; the launch traced here: 63 us
  Pallas kernels  59.1 us (93%)
  local copies, waits for them, and re-layouts  3.19 us (5%)
  between operations  0.65 us (1%)
    pallas_call x1, Pallas kernels, on_device(): pl.pallas_call(kernel, out_shape=(jax.ShapeDtypeStruct((32, 64, 256), BF1...  59.1 us
    unnamed x6, local copies, waits for them, and re-layouts  3.19 us

profile of v5, /device:TPU:0, one launch (start us, length us, event | category | flops | bytes accessed | tf_op | source)
XLA Modules:
  0.0 63.0 jit_solution(9007116589004960085)
XLA Ops:
  0.6 0.0 copy-start
  0.6 0.9 %copy-done = bf16[256,256]{1,0:T(8,128)(2,1)S(1)} copy-done((bf16[256,256]{1,0:T(8,128)(2,1)S(1)}, bf16[256,256]{1,0:T(8,128)(2,1)}, u32[]{:S(2)}) %copy-start) | copy-done | bytes 131096
  1.5 0.0 copy-start.1
  1.5 0.7 %copy-done.1 = f32[16,256]{1,0:T(8,128)S(1)} copy-done((f32[16,256]{1,0:T(8,128)S(1)}, f32[16,256]{1,0:T(8,128)}, u32[]{:S(2)}) %copy-start.1) | copy-done | bytes 16408
  2.3 59.1 %shard_map.59 = (bf16[32,64,256]{2,1,0:T(8,128)(2,1)S(1)}, f32[16,256]{1,0:T(8,128)S(1)}) custom-call(bf16[32,64,256]{2,1,0:T(8,128)(2,1)} %cot.1, bf16[32,64,256]{2,1,0:T(8,128)(2,1)} %field.1, bf16[256,256]{1,0:T(8,128)(2,1)S(1)} %copy-done, f32[16,256]{1,0:T(8,128)S(1)} %copy-done.1), custom_call_target="tpu_custom_call" | custom-call | tf_op jit(solution)/shard_map/pallas_call | solution.py:340
  61.4 1.0 %copy.8 = bf16[32,64,256]{2,1,0:T(8,128)(2,1)} copy(bf16[32,64,256]{2,1,0:T(8,128)(2,1)S(1)} %get-tuple-element.4) | data formatting | bytes 2097152
  62.4 0.6 copy.9
Async XLA Ops:
  0.6 0.9 %copy-start = (bf16[256,256]{1,0:T(8,128)(2,1)S(1)}, bf16[256,256]{1,0:T(8,128)(2,1)}, u32[]{:S(2)}) copy-start(bf16[256,256]{1,0:T(8,128)(2,1)} %temporal_in.1) | copy-start | bytes 393220
  1.5 0.7 %copy-start.1 = (f32[16,256]{1,0:T(8,128)S(1)}, f32[16,256]{1,0:T(8,128)}, u32[]{:S(2)}) copy-start(f32[16,256]{1,0:T(8,128)} %embed_in.1) | copy-start | bytes 49156
